TPU v7x, 32 devices: a whole 2x2x4 slice. The times are simulated.
32 devices in a mesh: dp: 8 (over z, x), mp: 4 (over y, core).
Axes of the slice: x: 2, y: 2, z: 4, core: 2. Of those that a mesh axis runs over, the one named last changes fastest.
Arguments:
- tokens: bfloat16 [32768, 1024], P(('dp', 'mp')), may hold values from -6 to 6
- lengths: int32 [32], P(('dp', 'mp')), may hold values from 10 to 1024, as said below
- key_mask: int32 [32768], P(('dp', 'mp')), may hold values 0 or 1
- w_query: bfloat16 [1024, 1024], replicated, may hold values from -0.1875 to 0.1875
- w_key: bfloat16 [1024, 1024], replicated, may hold values from -0.1875 to 0.1875
- w_value: bfloat16 [1024, 1024], replicated, may hold values from -0.1875 to 0.1875
- w_output: bfloat16 [1024, 1024], replicated, may hold values from -1.5 to 1.5
- norm1_gain: bfloat16 [1024], replicated, may hold values from 0.5 to 1.5
- norm1_shift: bfloat16 [1024], replicated, may hold values from -1.5 to 1.5
- w_in: bfloat16 [1024, 4096], P(None, 'mp'), may hold values from -0.1875 to 0.1875
- b_in: bfloat16 [4096], P('mp'), may hold values from -2.5 to 2.5
- w_out: bfloat16 [4096, 1024], P('mp'), may hold values from -0.09375 to 0.09375
- norm2_gain: bfloat16 [1024], replicated, may hold values from 0.5 to 1.5
- norm2_shift: bfloat16 [1024], replicated, may hold values from -1.5 to 1.5
- prefix_key: bfloat16 [64, 1024], replicated, may hold values from -6 to 6
- prefix_value: bfloat16 [64, 1024], replicated, may hold values from -6 to 6
- out_grad: bfloat16 [32768, 1024], P(('dp', 'mp')), may hold values from -6 to 6
Outputs:
- output: bfloat16 [32768, 1024], P(('dp', 'mp'))
- input_grad: bfloat16 [32768, 1024], P(('dp', 'mp'))
- prefix_key_grad: float32 [64, 1024], P(None, 'mp')
- prefix_value_grad: float32 [64, 1024], P(None, 'mp')
Inputs may be any that keep to these rules, and one draw needn't show every extreme that they name: `lengths`: some slot holds a sentence of exactly 1024 tokens and another one of exactly 10.
All inputs are finite; a program needn't handle non-finite values. No bound on the sum of `key_mask` on one device may be relied on, other than what follows from the above.
Results may differ from a plain program's by a relative error of at most 0.014.
Values may be sent and summed in bfloat16 or wider, within the bound.
A program may use at most 256 MiB of HBM per device.

v0:
```python
import math

import jax
import jax.numpy as jnp
from jax import lax
from jax.sharding import PartitionSpec as P

HEADS = 16
HEAD = 64
PREFIX = 64
SLOT = 1024


epsilon = 1e-05
masked_score = -1e30


def norm_rows(hidden_rows, gain, shift):
    middle = jnp.mean(hidden_rows, axis=-1, keepdims=True)
    centered = hidden_rows - middle
    spread = jnp.mean(centered * centered, axis=-1, keepdims=True)
    inverse = lax.rsqrt(spread + epsilon)
    unit = centered * inverse
    return (unit * gain + shift, unit, inverse)


def norm_back(grad, unit, inverse, gain):
    scaled = grad * gain
    first = jnp.mean(scaled, axis=-1, keepdims=True)
    second = jnp.mean(scaled * unit, axis=-1, keepdims=True)
    return inverse * (scaled - first - unit * second)


def gelu_slope(values):
    normal_part = 0.5 * (1.0 + lax.erf(values * (1.0 / math.sqrt(2.0))))
    return normal_part + values * jnp.exp(-0.5 * values * values) * (1.0 / math.sqrt(2.0 * math.pi))


def product(left, right):
    return jnp.dot(left, right, preferred_element_type=jnp.float32)


def product_back(left, right):
    return lax.dot_general(
        left, right, (((1,), (1,)), ((), ())), preferred_element_type=jnp.float32
    )


def block_scores(query_block, keys, live, scale):
    scores = (
        jnp.einsum("qhd,khd->hqk", query_block, keys, preferred_element_type=jnp.float32) * scale
    )
    return jnp.where(live[None, None, :], scores, masked_score)


def attend_forward(queries, keys, values, live, scale):

    def one_slot(item):
        slot_queries, slot_keys, slot_values, slot_live = item

        def one_block(query_block):
            scores = block_scores(query_block, slot_keys, slot_live, scale)
            peak = jnp.max(scores, axis=-1, keepdims=True)
            weights = jnp.exp(scores - peak)
            total = jnp.sum(weights, axis=-1, keepdims=True)
            probs = (weights / total).astype(jnp.bfloat16)
            context = jnp.einsum(
                "hqk,khd->qhd", probs, slot_values, preferred_element_type=jnp.float32
            )
            return (context.astype(jnp.bfloat16), peak[..., 0] + jnp.log(total[..., 0]))

        return lax.map(one_block, slot_queries)

    return lax.map(one_slot, (queries, keys, values, live))


def attend_back(queries, keys, values, live, context_grads, log_totals, scale):

    def one_slot(item):
        slot_queries, slot_keys, slot_values, slot_live, slot_grads, slot_totals = item

        def one_block(carry, block_item):
            key_sum, value_sum = carry
            query_block, grad_block, totals = block_item
            scores = block_scores(query_block, slot_keys, slot_live, scale)
            probs = jnp.exp(scores - totals[..., None])
            value_sum = value_sum + jnp.einsum(
                "hqk,qhd->khd",
                probs.astype(jnp.bfloat16),
                grad_block,
                preferred_element_type=jnp.float32,
            )
            prob_grad = jnp.einsum(
                "qhd,khd->hqk", grad_block, slot_values, preferred_element_type=jnp.float32
            )
            centre = jnp.sum(probs * prob_grad, axis=-1, keepdims=True)
            score_grad = (probs * (prob_grad - centre)).astype(jnp.bfloat16)
            query_grad = (
                jnp.einsum(
                    "hqk,khd->qhd", score_grad, slot_keys, preferred_element_type=jnp.float32
                )
                * scale
            )
            key_sum = (
                key_sum
                + jnp.einsum(
                    "hqk,qhd->khd", score_grad, query_block, preferred_element_type=jnp.float32
                )
                * scale
            )
            return ((key_sum, value_sum), query_grad.astype(jnp.bfloat16))

        zeros = jnp.zeros(slot_keys.shape, jnp.float32)
        (key_sum, value_sum), query_grads = lax.scan(
            one_block, (zeros, zeros), (slot_queries, slot_grads, slot_totals)
        )
        return (query_grads, key_sum, value_sum)

    return lax.map(one_slot, (queries, keys, values, live, context_grads, log_totals))


def local(
    tokens,
    lengths,
    key_mask,
    w_query,
    w_key,
    w_value,
    w_output,
    norm1_gain,
    norm1_shift,
    w_in,
    b_in,
    w_out,
    norm2_gain,
    norm2_shift,
    prefix_key,
    prefix_value,
    out_grad,
):
    rows = tokens.shape[0]
    width = tokens.shape[1]
    slot_count = lengths.shape[0]
    block_rows = min(512, SLOT)
    block_count = SLOT // block_rows
    scale = 1.0 / math.sqrt(HEAD)
    gain_one = norm1_gain.astype(jnp.float32)
    gain_two = norm2_gain.astype(jnp.float32)
    positions = jnp.arange(SLOT, dtype=jnp.int32)
    live_tokens = (positions[None, :] < lengths[:, None]) & (key_mask.reshape(slot_count, SLOT) > 0)
    live = jnp.concatenate([jnp.ones((slot_count, PREFIX), dtype=bool), live_tokens], axis=1)
    queries = product(tokens, w_query).astype(jnp.bfloat16)
    keys_own = product(tokens, w_key).astype(jnp.bfloat16)
    values_own = product(tokens, w_value).astype(jnp.bfloat16)

    def with_prefix(prefix, own):
        shared = prefix.reshape(1, PREFIX, HEADS, HEAD)
        return jnp.concatenate([shared, own.reshape(slot_count, SLOT, HEADS, HEAD)], axis=1)

    keys = with_prefix(prefix_key, keys_own)
    values = with_prefix(prefix_value, values_own)
    query_blocks = queries.reshape(slot_count, block_count, block_rows, HEADS, HEAD)
    context, log_totals = attend_forward(query_blocks, keys, values, live, scale)
    context = context.reshape(rows, width)
    mixed = tokens.astype(jnp.float32) + product(context, w_output)
    normed, unit_one, inverse_one = norm_rows(mixed, gain_one, norm1_shift.astype(jnp.float32))
    normed_low = normed.astype(jnp.bfloat16)
    gathered = lax.all_gather(normed_low, "mp", axis=0, tiled=True)
    pre = product(gathered, w_in) + b_in.astype(jnp.float32)
    active = jax.nn.gelu(pre, approximate=False).astype(jnp.bfloat16)
    ffn = lax.psum_scatter(
        product(active, w_out).astype(jnp.bfloat16), "mp", scatter_dimension=0, tiled=True
    ).astype(jnp.float32)
    summed = normed + ffn
    result, unit_two, inverse_two = norm_rows(summed, gain_two, norm2_shift.astype(jnp.float32))
    upper_grad = norm_back(out_grad.astype(jnp.float32), unit_two, inverse_two, gain_two)
    upper_low = upper_grad.astype(jnp.bfloat16)
    grad_rows = lax.all_gather(upper_low, "mp", axis=0, tiled=True)
    active_grad = product_back(grad_rows, w_out)
    pre_grad = (active_grad * gelu_slope(pre)).astype(jnp.bfloat16)
    ffn_back = lax.psum_scatter(
        product_back(pre_grad, w_in).astype(jnp.bfloat16), "mp", scatter_dimension=0, tiled=True
    ).astype(jnp.float32)
    lower_grad = norm_back(upper_grad + ffn_back, unit_one, inverse_one, gain_one)
    context_grad = product_back(lower_grad.astype(jnp.bfloat16), w_output).astype(jnp.bfloat16)
    grad_blocks = context_grad.reshape(slot_count, block_count, block_rows, HEADS, HEAD)
    query_grads, key_sums, value_sums = attend_back(
        query_blocks, keys, values, live, grad_blocks, log_totals, scale
    )
    query_grads = query_grads.reshape(rows, width)
    key_tokens = key_sums[:, PREFIX:].reshape(rows, width).astype(jnp.bfloat16)
    value_tokens = value_sums[:, PREFIX:].reshape(rows, width).astype(jnp.bfloat16)
    prefix_keys = jnp.sum(key_sums[:, :PREFIX], axis=0).reshape(PREFIX, width)
    prefix_values = jnp.sum(value_sums[:, :PREFIX], axis=0).reshape(PREFIX, width)
    input_grad = (
        lower_grad
        + product_back(query_grads, w_query)
        + product_back(key_tokens, w_key)
        + product_back(value_tokens, w_value)
    )
    key_whole, value_whole = lax.psum((prefix_keys, prefix_values), ("dp", "mp"))
    share_width = width // lax.axis_size("mp")
    offset = lax.axis_index("mp") * share_width
    key_grad = lax.dynamic_slice_in_dim(key_whole, offset, share_width, 1)
    value_grad = lax.dynamic_slice_in_dim(value_whole, offset, share_width, 1)
    return (result.astype(jnp.bfloat16), input_grad.astype(jnp.bfloat16), key_grad, value_grad)


def solution(mesh):
    in_specs = (
        P(("dp", "mp"), None),
        P(("dp", "mp")),
        P(("dp", "mp")),
        P(),
        P(),
        P(),
        P(),
        P(),
        P(),
        P(None, "mp"),
        P("mp"),
        P("mp", None),
        P(),
        P(),
        P(),
        P(),
        P(("dp", "mp"), None),
    )
    out_specs = (P(("dp", "mp"), None), P(("dp", "mp"), None), P(None, "mp"), P(None, "mp"))
    return jax.shard_map(local, mesh=mesh, in_specs=in_specs, out_specs=out_specs, check_vma=False)
```

profile of v0, /device:TPU:0, one launch (start us, length us, event | category | flops | bytes accessed | tf_op | source)
XLA Modules:
  0.0 934.5 jit_solution(3319712541195721313)
XLA Ops:
  11.3 6.1 convolution_convert_fusion.1
  27.5 6.3 reshape.133
  47.0 99.9 %while.47 = (s32[]{:T(128)}, bf16[2,512,16,64]{1,3,2,0:T(8,128)(2,1)}, f32[2,16,512]{2,1,0:T(8,128)S(1)}, pred[1088]{0:T(1024)(128)(4,1)S(1)}, bf16[2,512,16,64]...) while((s32[]{:T(128)}, ...), condition=%wide.region_3.4_spmd, body=%wide.region_0.3_spmd.sunk | while | flops 2389172224 | bytes 114037016 | solution.py:72
  47.1 17.5 %fusion.156 = (f32[16,512]{1,0:T(8,128)S(1)}, f32[16,512,1088]{1,2,0:T(8,128)}) fusion(pred[1088]{0:T(1024)(128)(4,1)S(1)} %get-tuple-element.410, bf16[1088,16,64]{0,2,1:T(8,128)(2,1)} %get-tuple-element.412, bf16[2,512,16,64]{1,3,2,0:T(8,128)(2,1)} %get-tuple-element.411, s32[]{:T(128)} %get-tuple-element.399), kind=kOutput, calls=%fused_computation.3.clone.1 | convolution fusion | flops 1167581184 | bytes 39093824 | tf_op jit(solution)/shard_map/while/body/eval_jaxpr/while/body/eval_jaxpr/qhd,khd->hqk/dot_general | solution.py:51
  64.6 15.1 %fusion.157 = f32[16,512]{1,0:T(8,128)S(1)} fusion(f32[16,512,1088]{1,2,0:T(8,128)} %get-tuple-element.377, f32[16,512]{1,0:T(8,128)S(1)} %get-tuple-element.378, pred[1088]{0:T(1024)(128)(4,1)S(1)} %get-tuple-element.410), kind=kLoop, calls=%fused_computation.4.clone.1 | loop fusion | flops 35643392 | bytes 35718208 | tf_op jit(solution)/shard_map/while/body/eval_jaxpr/while/body/eval_jaxpr/reduce_sum | solution.py:65
  79.7 17.2 %fusion.158 = bf16[2,512,16,64]{1,3,2,0:T(8,128)(2,1)} fusion(bf16[2,512,16,64]{1,3,2,0:T(8,128)(2,1)} %get-tuple-element.400, s32[]{:T(128)} %get-tuple-element.399, bf16[1088,16,64]{0,2,1:T(8,128)(2,1)} %get-tuple-element.413, f32[16,512,1088]{1,2,0:T(8,128)} %get-tuple-element.377, f32[16,512]{1,0:T(8,128)S(1)} %fusion.157, ...), kind=kOutput, calls=%fused_computation.8.clone.1 | convolution fusion | flops 1185939456 | bytes 39126592 | tf_op jit(solution)/shard_map/while/body/eval_jaxpr/while/body/eval_jaxpr/hqk,khd->qhd/dot_general | solution.py:67
  96.9 17.5 %fusion.156 = (f32[16,512]{1,0:T(8,128)S(1)}, f32[16,512,1088]{1,2,0:T(8,128)}) fusion(pred[1088]{0:T(1024)(128)(4,1)S(1)} %get-tuple-element.410, bf16[1088,16,64]{0,2,1:T(8,128)(2,1)} %get-tuple-element.412, bf16[2,512,16,64]{1,3,2,0:T(8,128)(2,1)} %get-tuple-element.411, s32[]{:T(128)} %get-tuple-element.399), kind=kOutput, calls=%fused_computation.3.clone.1 | convolution fusion | flops 1167581184 | bytes 39093824 | tf_op jit(solution)/shard_map/while/body/eval_jaxpr/while/body/eval_jaxpr/qhd,khd->hqk/dot_general | solution.py:51
  114.4 15.1 %fusion.157 = f32[16,512]{1,0:T(8,128)S(1)} fusion(f32[16,512,1088]{1,2,0:T(8,128)} %get-tuple-element.377, f32[16,512]{1,0:T(8,128)S(1)} %get-tuple-element.378, pred[1088]{0:T(1024)(128)(4,1)S(1)} %get-tuple-element.410), kind=kLoop, calls=%fused_computation.4.clone.1 | loop fusion | flops 35643392 | bytes 35718208 | tf_op jit(solution)/shard_map/while/body/eval_jaxpr/while/body/eval_jaxpr/reduce_sum | solution.py:65
  129.5 17.2 %fusion.158 = bf16[2,512,16,64]{1,3,2,0:T(8,128)(2,1)} fusion(bf16[2,512,16,64]{1,3,2,0:T(8,128)(2,1)} %get-tuple-element.400, s32[]{:T(128)} %get-tuple-element.399, bf16[1088,16,64]{0,2,1:T(8,128)(2,1)} %get-tuple-element.413, f32[16,512,1088]{1,2,0:T(8,128)} %get-tuple-element.377, f32[16,512]{1,0:T(8,128)S(1)} %fusion.157, ...), kind=kOutput, calls=%fused_computation.8.clone.1 | convolution fusion | flops 1185939456 | bytes 39126592 | tf_op jit(solution)/shard_map/while/body/eval_jaxpr/while/body/eval_jaxpr/hqk,khd->qhd/dot_general | solution.py:67
  158.1 61.1 %all-gather.3.cloned.1.call-done = bf16[4096,1024]{0,1:T(8,128)(2,1)} async-done(((bf16[1024,1024]{0,1:T(8,128)(2,1)}), bf16[4096,1024]{0,1:T(8,128)(2,1)}) %all-gather.3.cloned.1.call-update) | async-done | bytes 8388624 | tf_op jit(solution)/shard_map/all_gather | solution.py:168
  219.2 12.4 %fusion.107 = f32[4096,1024]{1,0:T(8,128)S(1)} fusion(bf16[4096,1024]{0,1:T(8,128)(2,1)} %all-gather.3.cloned.1.call-done, bf16[1024,1024]{1,0:T(8,128)(2,1)} %param.30), kind=kOutput, calls=%fused_computation.156 | convolution fusion | flops 8589934592 | bytes 27262976 | tf_op jit(solution)/shard_map/dot_general | solution.py:40
  237.4 51.9 %fusion.56 = bf16[4096,1024]{0,1:T(8,128)(2,1)} fusion(bf16[1024,1024]{1,0:T(8,128)(2,1)S(1)} %copy-done, f32[4096,1024]{1,0:T(8,128)S(1)} %fusion.107, f32[1024]{0:T(1024)S(1)} %convert_element_type.102), kind=kOutput, calls=%fused_computation.75 | convolution fusion | flops 8870952960 | bytes 27267072 | tf_op jit(solution)/shard_map/dot_general | solution.py:40
  293.3 67.9 %reduce-scatter.3.cloned.1.call-done = bf16[1024,1024]{0,1:T(8,128)(2,1)} async-done(((bf16[4096,1024]{0,1:T(8,128)(2,1)}), bf16[1024,1024]{0,1:T(8,128)(2,1)}) %reduce-scatter.3.cloned.1.call-update) | async-done | bytes 2097168 | tf_op jit(solution)/shard_map/reduce_scatter | solution.py:171
  371.4 58.4 %all-gather.5.cloned.1.call-done = bf16[4096,1024]{0,1:T(8,128)(2,1)} async-done(((bf16[1024,1024]{0,1:T(8,128)(2,1)}), bf16[4096,1024]{0,1:T(8,128)(2,1)}) %all-gather.5.cloned.1.call-update) | async-done | bytes 8388624 | tf_op jit(solution)/shard_map/all_gather | solution.py:178
  429.8 23.5 %fusion.59 = bf16[4096,1024]{0,1:T(8,128)(2,1)} fusion(bf16[1024,1024]{1,0:T(8,128)(2,1)} %param.30, f32[4096,1024]{1,0:T(8,128)} %copy-done.43, bf16[4096,1024]{0,1:T(8,128)(2,1)} %all-gather.5.cloned.1.call-done, bf16[1024,1024]{1,0:T(8,128)(2,1)S(1)} %copy-done, f32[1024]{0:T(1024)S(1)} %convert_element_type.102), kind=kOutput, calls=%fused_computation.76 | convolution fusion | flops 17230200832 | bytes 37752832 | tf_op jit(solution)/shard_map/dot_general | solution.py:44
  454.0 71.2 %reduce-scatter.5.cloned.1.call-done = bf16[1024,1024]{0,1:T(8,128)(2,1)} async-done(((bf16[4096,1024]{0,1:T(8,128)(2,1)}), bf16[1024,1024]{0,1:T(8,128)(2,1)}) %reduce-scatter.5.cloned.1.call-update) | async-done | bytes 2097168 | tf_op jit(solution)/shard_map/reduce_scatter | solution.py:181
  525.3 6.8 fusion.104
  547.7 227.3 %while.48 = (s32[]{:T(128)}, f32[1088,16,64]{0,2,1:T(8,128)}, f32[1088,16,64]{0,2,1:T(8,128)}, bf16[2,512,16,64]{1,3,2,0:T(8,128)(2,1)}, bf16[2,512,16,64]{1,3,2...) while((s32[]{:T(128)}, f32[1088,16,64]{0,2,1:T(8,128)}, ...), condition=%wide.region_16.17_spmd.clone, body=%wide.region_14.16_spmd.clone.sunk | while | flops 5791080448 | bytes 331647744 | solution.py:114
  547.9 18.6 %fusion.168 = f32[16,512,1088]{1,2,0:T(8,128)} fusion(bf16[1088,16,64]{0,2,1:T(8,128)(2,1)} %get-tuple-element.448, bf16[2,512,16,64]{1,3,2,0:T(8,128)(2,1)} %get-tuple-element.447, s32[]{:T(128)} %get-tuple-element.427), kind=kOutput, calls=%fused_computation.28.clone.1 | convolution fusion | flops 1140850688 | bytes 39059968 | tf_op jit(solution)/shard_map/while/body/eval_jaxpr/while/body/eval_jaxpr/qhd,khd->hqk/dot_general | solution.py:93
  566.5 27.4 %multiply_reduce_fusion.6 = (f32[16,512]{1,0:T(8,128)S(1)}, f32[16,512,1088]{1,2,0:T(8,128)}) fusion(f32[16,512,1088]{1,2,0:T(8,128)} %fusion.168, f32[16,512]{1,0:T(8,128)S(1)} %dynamic-slice_bitcast_fusion.2, bf16[1088,16,64]{0,2,1:T(8,128)(2,1)} %get-tuple-element.445, bf16[2,512,16,64]{1,3,2,0:T(8,128)(2,1)S(1)} %get-tuple-element.443, ...), kind=kOutput, calls=%fused_computation.17.clone.1 | convolution fusion | flops 1185406976 | bytes 74647552 | tf_op jit(solution)/shard_map/while/body/eval_jaxpr/while/body/eval_jaxpr/qhd,khd->hqk/dot_general | solution.py:51
  593.8 29.4 %multiply_convert_fusion.3 = bf16[16,512,1088]{1,2,0:T(8,128)(2,1)} fusion(f32[16,512,1088]{1,2,0:T(8,128)} %get-tuple-element.389, f32[16,512,1088]{1,2,0:T(8,128)} %fusion.168, f32[16,512]{1,0:T(8,128)S(1)} %get-tuple-element.390), kind=kLoop, calls=%fused_computation.16.clone.1 | loop fusion | flops 26738688 | bytes 89161728 | tf_op jit(solution)/shard_map/while/body/eval_jaxpr/while/body/eval_jaxpr/convert_element_type | solution.py:97
  623.3 10.6 %bitcast_add_fusion.4 = f32[1088,16,64]{0,2,1:T(8,128)} fusion(f32[1088,16,64]{0,2,1:T(8,128)} %get-tuple-element.428, bf16[16,512,1088]{1,2,0:T(8,128)(2,1)} %multiply_convert_fusion.3, pred[]{:T(512)S(6)} %compare.4, bf16[2,512,16,64]{1,3,2,0:T(8,128)(2,1)S(1)} %get-tuple-element.443, s32[]{:T(128)} %get-tuple-element.427), kind=kOutput, calls=%fused_computation.23.clone.1 | convolution fusion | flops 1144193024 | bytes 27787268 | tf_op jit(solution)/shard_map/while/body/eval_jaxpr/while/body/eval_jaxpr/hqk,qhd->khd/dot_general | solution.py:106
  633.8 9.5 %fusion.169 = bf16[2,512,16,64]{1,3,2,0:T(8,128)(2,1)S(1)} fusion(bf16[2,512,16,64]{1,3,2,0:T(8,128)(2,1)S(1)} %copy-done.11, s32[]{:T(128)} %get-tuple-element.427, bf16[1088,16,64]{0,2,1:T(8,128)(2,1)S(1)} %copy-done.2, bf16[16,512,1088]{1,2,0:T(8,128)(2,1)} %multiply_convert_fusion.3), kind=kOutput, calls=%fused_computation.26.clone.1 | convolution fusion | flops 1141899264 | bytes 21233668 | tf_op jit(solution)/shard_map/while/body/eval_jaxpr/while/body/eval_jaxpr/hqk,khd->qhd/dot_general | solution.py:99
  644.7 15.5 %bitcast_add_fusion.5 = f32[1088,16,64]{0,2,1:T(8,128)} fusion(f32[1088,16,64]{0,2,1:T(8,128)} %get-tuple-element.429, f32[16,512,1088]{1,2,0:T(8,128)} %get-tuple-element.389, pred[]{:T(512)S(6)} %compare.4, bf16[2,512,16,64]{1,3,2,0:T(8,128)(2,1)S(1)} %copy-done.6, s32[]{:T(128)} %get-tuple-element.427), kind=kOutput, calls=%fused_computation.22.clone.1 | convolution fusion | flops 1151991808 | bytes 45613060 | tf_op jit(solution)/shard_map/while/body/eval_jaxpr/while/body/eval_jaxpr/hqk,qhd->khd/dot_general | solution.py:87
  660.1 18.6 %fusion.168 = f32[16,512,1088]{1,2,0:T(8,128)} fusion(bf16[1088,16,64]{0,2,1:T(8,128)(2,1)} %get-tuple-element.448, bf16[2,512,16,64]{1,3,2,0:T(8,128)(2,1)} %get-tuple-element.447, s32[]{:T(128)} %get-tuple-element.427), kind=kOutput, calls=%fused_computation.28.clone.1 | convolution fusion | flops 1140850688 | bytes 39059968 | tf_op jit(solution)/shard_map/while/body/eval_jaxpr/while/body/eval_jaxpr/qhd,khd->hqk/dot_general | solution.py:93
  678.7 27.4 %multiply_reduce_fusion.6 = (f32[16,512]{1,0:T(8,128)S(1)}, f32[16,512,1088]{1,2,0:T(8,128)}) fusion(f32[16,512,1088]{1,2,0:T(8,128)} %fusion.168, f32[16,512]{1,0:T(8,128)S(1)} %dynamic-slice_bitcast_fusion.2, bf16[1088,16,64]{0,2,1:T(8,128)(2,1)} %get-tuple-element.445, bf16[2,512,16,64]{1,3,2,0:T(8,128)(2,1)S(1)} %get-tuple-element.443, ...), kind=kOutput, calls=%fused_computation.17.clone.1 | convolution fusion | flops 1185406976 | bytes 74647552 | tf_op jit(solution)/shard_map/while/body/eval_jaxpr/while/body/eval_jaxpr/qhd,khd->hqk/dot_general | solution.py:51
  706.1 29.4 %multiply_convert_fusion.3 = bf16[16,512,1088]{1,2,0:T(8,128)(2,1)} fusion(f32[16,512,1088]{1,2,0:T(8,128)} %get-tuple-element.389, f32[16,512,1088]{1,2,0:T(8,128)} %fusion.168, f32[16,512]{1,0:T(8,128)S(1)} %get-tuple-element.390), kind=kLoop, calls=%fused_computation.16.clone.1 | loop fusion | flops 26738688 | bytes 89161728 | tf_op jit(solution)/shard_map/while/body/eval_jaxpr/while/body/eval_jaxpr/convert_element_type | solution.py:97
  735.5 11.7 %bitcast_add_fusion.4 = f32[1088,16,64]{0,2,1:T(8,128)} fusion(f32[1088,16,64]{0,2,1:T(8,128)} %get-tuple-element.428, bf16[16,512,1088]{1,2,0:T(8,128)(2,1)} %multiply_convert_fusion.3, pred[]{:T(512)S(6)} %compare.4, bf16[2,512,16,64]{1,3,2,0:T(8,128)(2,1)S(1)} %get-tuple-element.443, s32[]{:T(128)} %get-tuple-element.427), kind=kOutput, calls=%fused_computation.23.clone.1 | convolution fusion | flops 1144193024 | bytes 27787268 | tf_op jit(solution)/shard_map/while/body/eval_jaxpr/while/body/eval_jaxpr/hqk,qhd->khd/dot_general | solution.py:106
  747.2 9.5 %fusion.169 = bf16[2,512,16,64]{1,3,2,0:T(8,128)(2,1)S(1)} fusion(bf16[2,512,16,64]{1,3,2,0:T(8,128)(2,1)S(1)} %copy-done.11, s32[]{:T(128)} %get-tuple-element.427, bf16[1088,16,64]{0,2,1:T(8,128)(2,1)S(1)} %copy-done.2, bf16[16,512,1088]{1,2,0:T(8,128)(2,1)} %multiply_convert_fusion.3), kind=kOutput, calls=%fused_computation.26.clone.1 | convolution fusion | flops 1141899264 | bytes 21233668 | tf_op jit(solution)/shard_map/while/body/eval_jaxpr/while/body/eval_jaxpr/hqk,khd->qhd/dot_general | solution.py:99
  758.0 16.7 %bitcast_add_fusion.5 = f32[1088,16,64]{0,2,1:T(8,128)} fusion(f32[1088,16,64]{0,2,1:T(8,128)} %get-tuple-element.429, f32[16,512,1088]{1,2,0:T(8,128)} %get-tuple-element.389, pred[]{:T(512)S(6)} %compare.4, bf16[2,512,16,64]{1,3,2,0:T(8,128)(2,1)S(1)} %copy-done.6, s32[]{:T(128)} %get-tuple-element.427), kind=kOutput, calls=%fused_computation.22.clone.1 | convolution fusion | flops 1151991808 | bytes 45613060 | tf_op jit(solution)/shard_map/while/body/eval_jaxpr/while/body/eval_jaxpr/hqk,qhd->khd/dot_general | solution.py:87
  796.4 11.5 %add_convert_fusion = bf16[1024,1024]{0,1:T(8,128)(2,1)} fusion(f32[1024,1024]{0,1:T(8,128)} %fusion.109, f32[1024,1024]{0,1:T(8,128)} %fusion.108, bf16[1024,1024]{1,0:T(8,128)(2,1)} %param.26, bf16[1024,1024]{0,1:T(8,128)(2,1)} %bitcast.133, f32[1024]{0:T(1024)S(1)} %copy-done.30, f32[1024,1024]{0,1:T(8,128)} %copy-done.7, f32[1024]{0:T(1024)S(1)} %copy-done.25, ...), kind=kOutput, calls=%fused_computation.79 | convolution fusion | flops 2157969408 | bytes 23085056 | tf_op jit(solution)/shard_map/dot_general | solution.py:44
  815.8 108.8 %all-reduce.4.cloned.1.call-done = (f32[64,1024]{1,0:T(8,128)}, f32[64,1024]{1,0:T(8,128)}) async-done(((f32[64,1024]{1,0:T(8,128)}, f32[64,1024]{1,0:T(8,128)}), (f32[64,1024]{1,0:T(8,128)}, f32[64,1024]{1,0:T(8,128)})) %all-reduce.4.cloned.1.call-update) | async-done | bytes 524304 | tf_op jit(solution)/shard_map/psum | solution.py:201
  (165 shorter events, 108.6 us)
Async XLA Ops:
  7.2 230.2 %copy-start = (bf16[1024,1024]{1,0:T(8,128)(2,1)S(1)}, bf16[1024,1024]{1,0:T(8,128)(2,1)}, u32[]{:S(2)}) copy-start(bf16[1024,1024]{1,0:T(8,128)(2,1)} %param.32) | copy-start | bytes 6291460
  7.2 212.0 %all-gather.3.cloned.1.call-start = ((), (), s32[]{:S(2)}) async-start(), calls=%async_computation.2 | async-start | bytes 10485760 | tf_op jit(solution)/shard_map/all_gather | solution.py:168
  11.3 6.1 copy-start.15
  11.3 6.1 copy-start.42
  33.8 6.1 copy-start.28
  146.9 4.5 copy-start.18
  146.9 4.5 copy-start.20
  146.9 4.5 copy-start.16
  147.0 4.5 copy-start.38
  154.1 378.0 %copy-start.24 = (f32[1024]{0:T(1024)}, f32[1024]{0:T(1024)S(1)}, u32[]{:S(2)}) copy-start(f32[1024]{0:T(1024)S(1)} %broadcast_multiply_fusion.5) | copy-start | bytes 12292
  154.8 377.3 %copy-start.26 = (f32[1024]{0:T(1024)}, f32[1024]{0:T(1024)S(1)}, u32[]{:S(2)}) copy-start(f32[1024]{0:T(1024)S(1)} %add_rsqrt_fusion.1) | copy-start | bytes 12292
  158.1 203.1 %reduce-scatter.3.cloned.1.call-start = ((), (), s32[]{:S(2)}) async-start(), calls=%async_computation.3 | async-start | bytes 10485760 | tf_op jit(solution)/shard_map/reduce_scatter | solution.py:171
  231.6 5.7 copy-start.43
  289.3 140.5 %all-gather.5.cloned.1.call-start = ((), (), s32[]{:S(2)}) async-start(), calls=%async_computation.4 | async-start | bytes 10485760 | tf_op jit(solution)/shard_map/all_gather | solution.py:178
  371.4 153.9 %reduce-scatter.5.cloned.1.call-start = ((), (), s32[]{:S(2)}) async-start(), calls=%async_computation.5 | async-start | bytes 10485760 | tf_op jit(solution)/shard_map/reduce_scatter | solution.py:181
  453.3 71.9 %copy-start.10 = (bf16[1024,1024]{0,1:T(8,128)(2,1)S(1)}, bf16[1024,1024]{0,1:T(8,128)(2,1)}, u32[]{:S(2)}) copy-start(bf16[1024,1024]{0,1:T(8,128)(2,1)} %copy.44) | copy-start | bytes 6291460
  453.4 471.2 %all-reduce.4.cloned.1.call-start = ((), (), s32[]{:S(2)}) async-start(), calls=%async_computation.6 | async-start | bytes 1048576 | tf_op jit(solution)/shard_map/psum | solution.py:201
  525.3 8.7 copy-start.8
  525.3 8.7 copy-start.39
  532.0 4.5 copy-start.29
  540.5 7.2 copy-start.4
  540.5 7.2 copy-start.19
  540.5 7.2 copy-start.21
  623.3 10.6 %copy-start.2 = (bf16[1088,16,64]{0,2,1:T(8,128)(2,1)S(1)}, bf16[1088,16,64]{0,2,1:T(8,128)(2,1)}, u32[]{:S(2)}) copy-start(bf16[1088,16,64]{0,2,1:T(8,128)(2,1)} %get-tuple-element.445) | copy-start | bytes 6684676 | tf_op jit(solution)/shard_map/while/body/eval_jaxpr/while
  623.3 10.6 %copy-start.11 = (bf16[2,512,16,64]{1,3,2,0:T(8,128)(2,1)S(1)}, bf16[2,512,16,64]{1,3,2,0:T(8,128)(2,1)}, u32[]{:S(2)}) copy-start(bf16[2,512,16,64]{1,3,2,0:T(8,128)(2,1)} %get-tuple-element.430) | copy-start | bytes 6291460 | tf_op jit(solution)/shard_map/while/body/eval_jaxpr/while
  633.8 10.8 %copy-start.6 = (bf16[2,512,16,64]{1,3,2,0:T(8,128)(2,1)S(1)}, bf16[2,512,16,64]{1,3,2,0:T(8,128)(2,1)}, u32[]{:S(2)}) copy-start(bf16[2,512,16,64]{1,3,2,0:T(8,128)(2,1)} %get-tuple-element.447) | copy-start | bytes 6291460 | tf_op jit(solution)/shard_map/while/body/eval_jaxpr/while
  735.5 11.7 %copy-start.2 = (bf16[1088,16,64]{0,2,1:T(8,128)(2,1)S(1)}, bf16[1088,16,64]{0,2,1:T(8,128)(2,1)}, u32[]{:S(2)}) copy-start(bf16[1088,16,64]{0,2,1:T(8,128)(2,1)} %get-tuple-element.445) | copy-start | bytes 6684676 | tf_op jit(solution)/shard_map/while/body/eval_jaxpr/while
  735.5 11.7 %copy-start.11 = (bf16[2,512,16,64]{1,3,2,0:T(8,128)(2,1)S(1)}, bf16[2,512,16,64]{1,3,2,0:T(8,128)(2,1)}, u32[]{:S(2)}) copy-start(bf16[2,512,16,64]{1,3,2,0:T(8,128)(2,1)} %get-tuple-element.430) | copy-start | bytes 6291460 | tf_op jit(solution)/shard_map/while/body/eval_jaxpr/while
  747.2 10.8 %copy-start.6 = (bf16[2,512,16,64]{1,3,2,0:T(8,128)(2,1)S(1)}, bf16[2,512,16,64]{1,3,2,0:T(8,128)(2,1)}, u32[]{:S(2)}) copy-start(bf16[2,512,16,64]{1,3,2,0:T(8,128)(2,1)} %get-tuple-element.447) | copy-start | bytes 6291460 | tf_op jit(solution)/shard_map/while/body/eval_jaxpr/while
  775.0 5.9 copy-start.3
  787.6 4.4 copy-start.17
  796.4 131.1 %copy-start.1 = (bf16[1024,1024]{1,0:T(8,128)(2,1)S(1)}, bf16[1024,1024]{1,0:T(8,128)(2,1)}, u32[]{:S(2)}) copy-start(bf16[1024,1024]{1,0:T(8,128)(2,1)} %param.32) | copy-start | bytes 6291460
  (21 other events, 60.3 us)
Sparse Core Ops, SparseCore 0:
  158.2 60.9 all-gather.2
  289.4 71.7 reduce-scatter.2
  371.5 58.2 all-gather.4
  453.5 71.7 reduce-scatter.4
  796.4 128.0 all-reduce.3
where the time goes:
time: 943 us; the launch traced here: 934 us
  waiting for transfers between devices  367 us (39%)
  matrix products  364 us (39%)
  other arithmetic  111 us (12%)
  local copies, waits for them, and re-layouts  75.9 us (8%)
  between operations  15.4 us (2%)
    psum x1, waiting for transfers between devices, local(): lax.psum((prefix_keys, prefix_values), ('dp', 'mp'))  109 us
    dot_general x4, matrix products, block_scores(): jnp.einsum('qhd,khd->hqk', query_block, keys, preferred_element_type=jnp....  89.8 us
    dot_general x6, matrix products, product(): return jnp.dot(left, right, preferred_element_type=jnp.float32)  82.6 us
    reduce_scatter x1, waiting for transfers between devices, local(): lax.psum_scatter(product_back(pre_grad, w_in).astype(jnp.bfloat16), 'mp',...  71.2 us
    reduce_scatter x1, waiting for transfers between devices, local(): lax.psum_scatter(product(active, w_out).astype(jnp.bfloat16), 'mp', scatt...  67.9 us
    all_gather x1, waiting for transfers between devices, local(): gathered = lax.all_gather(normed_low, 'mp', axis=0, tiled=True)  61.1 us
    convert_element_type x2, other arithmetic, one_block(): score_grad = (probs * (prob_grad - centre)).astype(jnp.bfloat16)  58.8 us
    all_gather x1, waiting for transfers between devices, local(): grad_rows = lax.all_gather(upper_low, 'mp', axis=0, tiled=True)  58.4 us
  transfers between devices with their start and end apart: 5, of which 5 were waited for; matrix products, arithmetic and copies ran while one was open for 3% of the time, Pallas kernels for 0%

commit v1 on v0

v1 whole, which is shorter than its diff:
```python
import functools
import math

import jax
import jax.numpy as jnp
from jax import lax
from jax.experimental import pallas as pl
from jax.experimental.pallas import tpu as pltpu
from jax.sharding import PartitionSpec as P

HEADS = 16
HEAD = 64
PREFIX = 64
SLOT = 1024
GROUP = 4
TILE = 256

EPSILON = 1e-05
MASKED = -1e30
LOG2E = 1.4426950408889634
BF = jnp.bfloat16
F32 = jnp.float32

VMEM = pl.BlockSpec(memory_space=pltpu.VMEM)
SMEM = pl.BlockSpec(memory_space=pltpu.SMEM)
HBM = pl.BlockSpec(memory_space=pl.ANY)


def dg(left, right, left_dim, right_dim):
    return lax.dot_general(
        left, right, (((left_dim,), (right_dim,)), ((), ())), preferred_element_type=F32
    )


def rows_at(start, size):
    return pl.ds(pl.multiple_of(start, size), size)


def block_diagonal(part):
    stacked = jnp.concatenate([part] * GROUP, axis=0)
    head_of_row = lax.broadcasted_iota(jnp.int32, stacked.shape, 0) // HEAD
    head_of_column = lax.broadcasted_iota(jnp.int32, stacked.shape, 1) // HEAD
    return jnp.where(head_of_row == head_of_column, stacked, jnp.zeros_like(stacked))


def diagonal_rows(blocks):
    head_of_row = lax.broadcasted_iota(jnp.int32, blocks.shape, 0) // HEAD
    head_of_column = lax.broadcasted_iota(jnp.int32, blocks.shape, 1) // HEAD
    kept = jnp.where(head_of_row == head_of_column, blocks, jnp.zeros_like(blocks))
    return kept[:64] + kept[64:128] + kept[128:192] + kept[192:]


def ones_rows(width):
    row = lax.broadcasted_iota(jnp.int32, (16, width), 0)
    return jnp.where(row == 0, 1.0, 0.0).astype(BF)


def project(tokens, w_query, w_key, w_value, query_t, key, key_t, value, value_t):
    width = tokens.shape[1]

    @pl.loop(0, width // TILE)
    def _(j):
        cols = rows_at(j * TILE, TILE)
        part = jnp.dot(tokens[...], w_query[:, cols], preferred_element_type=F32)
        query_t[cols, :] = (part * (LOG2E / math.sqrt(HEAD))).astype(BF).T
        part = jnp.dot(tokens[...], w_key[:, cols], preferred_element_type=F32).astype(BF)
        key[:, cols] = part
        key_t[cols, :] = part.T
        part = jnp.dot(tokens[...], w_value[:, cols], preferred_element_type=F32).astype(BF)
        value[:, cols] = part
        value_t[cols, :] = part.T


def mask_block(length, mask_ref, mask_cols):
    place = lax.broadcasted_iota(jnp.int32, (1, SLOT), 1)
    live = (place < length) & (mask_ref[...] > 0)
    bias = jnp.where(live, 0.0, MASKED)
    row = lax.broadcasted_iota(jnp.int32, (128, SLOT), 0)
    mask_cols[...] = jnp.where(row == 0, bias, 0.0).T.astype(BF)


def attend(query_t, key, value_t, mask_cols, prefix_key, prefix_value, weights_hbm, weights_prefix,
           context_t, inverse, scores_a, scores_b, scores_prefix, peak_prefix, peaks, sums, totals,
           weights_a, weights_b, sems):
    tiles = SLOT // TILE
    pairs = HEADS // 2

    @pl.loop(0, HEADS // GROUP)
    def _(g):
        cols = rows_at(g * 256, 256)
        s = jnp.dot(block_diagonal(prefix_key[:, cols]), query_t[cols, :], preferred_element_type=F32)
        scores_prefix[cols, :] = s
        peak_prefix[g] = jnp.concatenate(
            [jnp.max(s[i * 64 : i * 64 + 64], axis=0, keepdims=True) for i in range(GROUP)]
            + [jnp.zeros((4, SLOT), F32)], axis=0)

    def right_side(h, half):
        q = query_t[rows_at(h * HEAD, HEAD), :]
        zero = jnp.zeros_like(q)
        last = jnp.concatenate([ones_rows(SLOT), jnp.zeros((112, SLOT), BF)], axis=0)
        return jnp.concatenate([q, zero, last] if half == 0 else [zero, q, last], axis=0)

    def score_tile(h, t, right):
        rows = slice(t * TILE, (t + 1) * TILE)
        left = jnp.concatenate([key[rows, rows_at((h // 2) * 128, 128)], mask_cols[rows, :]], axis=1)
        return jnp.dot(left, right, preferred_element_type=F32)

    def folded(s):
        return jnp.max(s.reshape(TILE // 8, 8, SLOT), axis=0)

    def set_peak(h, half, peak):
        group = peak_prefix[h // GROUP]
        row = lax.broadcasted_iota(jnp.int32, group.shape, 0)
        own = jnp.max(jnp.where(row == h % GROUP, group, -jnp.inf), axis=0, keepdims=True)
        peaks[half : half + 1, :] = jnp.maximum(jnp.max(peak, axis=0, keepdims=True), own)

    def head_step(h, half, scores_new, scores_old, staged, more):
        if more:
            right = right_side(h + 1, 1 - half)
        top = peaks[half : half + 1, :]
        rows_h = rows_at(h * HEAD, HEAD)
        left = jnp.concatenate([value_t[rows_h, :], ones_rows(SLOT)], axis=0)
        total = jnp.zeros((80, SLOT), F32)
        peak = None
        for t in range(tiles):
            rows = slice(t * TILE, (t + 1) * TILE)
            if more:
                s = score_tile(h + 1, t, right)
                scores_new[rows, :] = s
                f = folded(s)
                peak = f if peak is None else jnp.maximum(peak, f)
            p = jnp.exp2(scores_old[rows, :] - top).astype(BF)
            staged[rows, :] = p
            total += jnp.dot(left[:, rows], p, preferred_element_type=F32)
        weights_prefix[rows_h, :] = jnp.exp2(scores_prefix[rows_h, :] - top).astype(BF)
        if more:
            set_peak(h + 1, 1 - half, peak)
        sums[rows_h, :] = total[:HEAD]
        totals[pl.ds(h, 1), :] = total[HEAD : HEAD + 1]

    right = right_side(0, 0)
    peak = None
    for t in range(tiles):
        s = score_tile(0, t, right)
        scores_a[t * TILE : (t + 1) * TILE, :] = s
        f = folded(s)
        peak = f if peak is None else jnp.maximum(peak, f)
    set_peak(0, 0, peak)

    def copy_out(h, half):
        return pltpu.make_async_copy((weights_a, weights_b)[half], weights_hbm.at[h], sems.at[half])

    @pl.loop(0, pairs - 1)
    def _(i):
        h = i * 2
        for half in range(2):
            @pl.when(i > 0)
            def _():
                copy_out(h + half - 2, half).wait()
            if half == 0:
                head_step(h, 0, scores_b, scores_a, weights_a, True)
            else:
                head_step(h + 1, 1, scores_a, scores_b, weights_b, True)
            copy_out(h + half, half).start()

    h = HEADS - 2
    copy_out(h - 2, 0).wait()
    head_step(h, 0, scores_b, scores_a, weights_a, True)
    copy_out(h, 0).start()
    copy_out(h - 1, 1).wait()
    head_step(h + 1, 1, scores_a, scores_b, weights_b, False)
    copy_out(h + 1, 1).start()

    @pl.loop(0, HEADS // GROUP)
    def _(g):
        cols = rows_at(g * 256, 256)
        head_of_row = lax.broadcasted_iota(jnp.int32, (256, 128), 0) // HEAD
        head_of_column = lax.broadcasted_iota(jnp.int32, (256, 128), 1)
        counts = jnp.where(head_of_row == head_of_column, 1.0, 0.0).astype(BF)
        left = jnp.concatenate([block_diagonal(prefix_value[:, cols]), counts], axis=1)
        both = dg(left, weights_prefix[cols, :], 0, 0)
        for i in range(GROUP):
            h = g * GROUP + i
            scale = 1.0 / (totals[pl.ds(h, 1), :] + both[256 + i : 257 + i, :])
            inverse[pl.ds(h, 1), :] = scale
            rows_h = rows_at(h * HEAD, HEAD)
            context_t[rows_h, :] = (
                (sums[rows_h, :] + both[i * HEAD : (i + 1) * HEAD]) * scale
            ).astype(BF)

    copy_out(HEADS - 2, 0).wait()
    copy_out(HEADS - 1, 1).wait()


def forward_kernel(length, mask_ref, tokens, w_query, w_key, w_value, prefix_key, prefix_value,
                   weights_hbm, weights_prefix, query_t, key_t, value, context_t, inverse,
                   key, value_t, mask_cols, scores_a, scores_b, scores_prefix, peak_prefix, peaks,
                   sums, totals, weights_a, weights_b, sems):
    mask_block(length[0], mask_ref, mask_cols)
    project(tokens, w_query, w_key, w_value, query_t, key, key_t, value, value_t)
    attend(query_t, key, value_t, mask_cols, prefix_key, prefix_value, weights_hbm, weights_prefix,
           context_t, inverse, scores_a, scores_b, scores_prefix, peak_prefix, peaks, sums, totals,
           weights_a, weights_b, sems)


def norm_parts(rows):
    centered = rows - jnp.mean(rows, axis=-1, keepdims=True)
    spread = jnp.mean(centered * centered, axis=-1, keepdims=True)
    inverse = lax.rsqrt(spread + EPSILON)
    return centered * inverse, inverse


def norm_back(scaled, unit, inverse):
    first = jnp.mean(scaled, axis=-1, keepdims=True)
    second = jnp.mean(scaled * unit, axis=-1, keepdims=True)
    return inverse * (scaled - first - unit * second)


def gelu_parts(v):
    u = v * (1.0 / math.sqrt(2.0))
    normal = 0.5 * lax.erf(u) + 0.5
    bell = jnp.exp2((u * u) * (-LOG2E))
    return (v * normal).astype(BF), (normal + (u * bell) * (1.0 / math.sqrt(math.pi))).astype(BF)


def middle_kernel(tokens, context_t, inverse, w_output, vectors, w_in, b_in, w_out, out_grad,
                  output, lower, grad_t, centre,
                  unit, inverse_one, low, total, active, slope):
    shards, width, hidden = w_in.shape
    rows = tokens.shape[0]
    gain_one, shift_one = vectors[0:1, :], vectors[1:2, :]
    gain_two, shift_two = vectors[2:3, :], vectors[3:4, :]

    @pl.loop(0, rows // TILE)
    def _(r):
        rs = rows_at(r * TILE, TILE)
        mixed = tokens[rs, :].astype(F32) + dg(context_t[:, rs], w_output[...], 0, 0)
        u, inv = norm_parts(mixed)
        unit[rs, :] = u
        inverse_one[rs, :] = inv
        normed = u * gain_one + shift_one
        total[rs, :] = normed
        low[rs, :] = normed.astype(BF)

    def first_parts(j):
        def part(c):
            cols = slice(c * TILE, (c + 1) * TILE)
            pre = jnp.dot(low[...], w_in[j, :, cols], preferred_element_type=F32) + b_in[j, 0:1, cols]
            act, slo = gelu_parts(pre)
            active[j % 2, :, cols] = act
            slope[j, :, cols] = slo
        return [functools.partial(part, c) for c in range(hidden // TILE)]

    def second_parts(j):
        def part(c):
            cols = slice(c * TILE, (c + 1) * TILE)
            total[:, cols] += jnp.dot(active[j % 2], w_out[j, :, cols], preferred_element_type=F32)
        return [functools.partial(part, c) for c in range(width // TILE)]

    def run(*lists):
        for k in range(max(len(parts) for parts in lists)):
            for parts in lists:
                if k < len(parts):
                    parts[k]()

    run(first_parts(0))

    @pl.loop(1, shards)
    def _(j):
        run(first_parts(j), second_parts(j - 1))

    run(second_parts(shards - 1))

    @pl.loop(0, rows // TILE)
    def _(r):
        rs = rows_at(r * TILE, TILE)
        u, inv = norm_parts(total[rs, :])
        output[rs, :] = (u * gain_two + shift_two).astype(BF)
        upper = norm_back(out_grad[rs, :].astype(F32) * gain_two, u, inv)
        total[rs, :] = upper
        low[rs, :] = upper.astype(BF)

    def third_parts(j):
        def part(c):
            cols = slice(c * TILE, (c + 1) * TILE)
            grad = dg(low[...], w_out[j, cols, :], 1, 1)
            active[j % 2, :, cols] = (grad * slope[j, :, cols].astype(F32)).astype(BF)
        return [functools.partial(part, c) for c in range(hidden // TILE)]

    def fourth_parts(j):
        def part(c):
            cols = slice(c * TILE, (c + 1) * TILE)
            total[:, cols] += dg(active[j % 2], w_in[j, cols, :], 1, 1)
        return [functools.partial(part, c) for c in range(width // TILE)]

    run(third_parts(0))

    @pl.loop(1, shards)
    def _(j):
        run(third_parts(j), fourth_parts(j - 1))

    run(fourth_parts(shards - 1))

    @pl.loop(0, rows // TILE)
    def _(r):
        rs = rows_at(r * TILE, TILE)
        grad = norm_back(total[rs, :] * gain_one, unit[rs, :], inverse_one[rs, :])
        lower[rs, :] = grad
        low[rs, :] = grad.astype(BF)

    @pl.loop(0, width // TILE)
    def _(g):
        gs = rows_at(g * TILE, TILE)
        grad = dg(w_output[gs, :], low[...], 1, 1)
        for i in range(TILE // HEAD):
            h = g * (TILE // HEAD) + i
            rows_h = rows_at(h * HEAD, HEAD)
            scaled = grad[i * HEAD : (i + 1) * HEAD] * inverse[pl.ds(h, 1), :]
            grad_t[rows_h, :] = scaled.astype(BF)
            middle = -jnp.sum(scaled * context_t[rows_h, :].astype(F32), axis=0, keepdims=True)
            high = middle.astype(BF)
            rest = (middle - high.astype(F32)).astype(BF)
            row = lax.broadcasted_iota(jnp.int32, (16, SLOT), 0)
            both = jnp.where(row == 0, high.astype(F32), jnp.where(row == 1, rest.astype(F32), 0.0))
            centre[rows_at(h * 16, 16), :] = both.astype(BF)


def backward_kernel(weights_hbm, weights_prefix, query_t, key_t, value, grad_t, centre, prefix_key,
                    prefix_value, lower, w_query, w_key, w_value,
                    input_grad, prefix_grads,
                    query_back, key_back, value_back, query_prefix, staged, sems):
    tiles = SLOT // TILE
    ln2 = 1.0 / LOG2E

    def copy_in(h, half):
        return pltpu.make_async_copy(weights_hbm.at[h], staged.at[half], sems.at[half])

    copy_in(0, 0).start()

    @pl.loop(0, HEADS // GROUP)
    def _(g):
        cols = rows_at(g * 256, 256)
        keys = block_diagonal(prefix_key[:, cols])
        values = block_diagonal(prefix_value[:, cols])
        grads = grad_t[cols, :]
        back = jnp.dot(values, grads, preferred_element_type=F32)
        parts = []
        for i in range(GROUP):
            middle = jnp.sum(centre[rows_at((g * GROUP + i) * 16, 16), :].astype(F32), axis=0, keepdims=True)
            rows_h = rows_at((g * GROUP + i) * HEAD, HEAD)
            parts.append(
                (weights_prefix[rows_h, :].astype(F32) * (back[i * HEAD : (i + 1) * HEAD] + middle)).astype(BF)
            )
        back = jnp.concatenate(parts, axis=0)
        prefix_grads[:PREFIX, cols] = diagonal_rows(dg(back, query_t[cols, :], 1, 1)) * ln2
        prefix_grads[PREFIX:, cols] = diagonal_rows(dg(weights_prefix[cols, :], grads, 1, 1))
        query_prefix[cols, :] = dg(keys, back, 0, 0)

    lane = lax.broadcasted_iota(jnp.int32, (TILE, 128), 1)
    pick = jnp.where(lane < 2, 1.0, 0.0).astype(BF)

    def head_step(h, half):
        rows_h = rows_at(h * HEAD, HEAD)
        pair = rows_at((h // 2) * 128, 128)
        grads = grad_t[rows_h, :]
        zero = jnp.zeros_like(grads)
        last = jnp.concatenate([centre[rows_at(h * 16, 16), :], jnp.zeros((112, SLOT), BF)], axis=0)
        right = jnp.concatenate([grads, zero, last] if half == 0 else [zero, grads, last], axis=0)
        queries = query_t[rows_h, :]
        keys = key_t[rows_h, :]
        total = query_prefix[rows_h, :]
        for t in range(tiles):
            rows = slice(t * TILE, (t + 1) * TILE)
            left = jnp.concatenate([value[rows, pair], pick], axis=1)
            back = jnp.dot(left, right, preferred_element_type=F32)
            w = staged[half, rows, :]
            back = (back * w.astype(F32)).astype(BF)
            value_back[rows_h, rows] = dg(grads, w, 1, 1).astype(BF)
            key_back[rows_h, rows] = (dg(queries, back, 1, 1) * ln2).astype(BF)
            total += jnp.dot(keys[:, rows], back, preferred_element_type=F32)
        query_back[rows_h, :] = (total * (1.0 / math.sqrt(HEAD))).astype(BF)

    @pl.loop(0, HEADS // 2)
    def _(i):
        h = i * 2
        copy_in(h, 0).wait()
        copy_in(h + 1, 1).start()
        head_step(h, 0)
        copy_in(h + 1, 1).wait()

        @pl.when(i < HEADS // 2 - 1)
        def _():
            copy_in(h + 2, 0).start()
        head_step(h + 1, 1)

    @pl.loop(0, SLOT // TILE)
    def _(r):
        rs = rows_at(r * TILE, TILE)
        grad = lower[rs, :]
        grad += dg(query_back[:, rs], w_query[...], 0, 1)
        grad += dg(key_back[:, rs], w_key[...], 0, 1)
        grad += dg(value_back[:, rs], w_value[...], 0, 1)
        input_grad[rs, :] = grad.astype(BF)


def local(tokens, lengths, key_mask, w_query, w_key, w_value, w_output, norm1_gain, norm1_shift,
          w_in, b_in, w_out, norm2_gain, norm2_shift, prefix_key, prefix_value, out_grad):
    rows, width = tokens.shape
    hidden = w_in.shape[1]
    shards = lax.axis_size("mp")
    shape = jax.ShapeDtypeStruct
    params = pltpu.CompilerParams(vmem_limit_bytes=60 * 2**20)

    w_in_all = lax.all_gather(w_in, "mp", axis=0)
    w_out_all = lax.all_gather(w_out, "mp", axis=0)
    b_all = lax.all_gather(jnp.broadcast_to(b_in.astype(F32)[None, :], (8, hidden)), "mp", axis=0)

    square = shape((SLOT, width), BF)
    weights, weights_prefix, query_t, key_t, value, context_t, inverse = pl.pallas_call(
        forward_kernel,
        out_shape=[shape((HEADS, SLOT, SLOT), BF), square, square, square, square, square,
                   shape((HEADS, SLOT), F32)],
        in_specs=[SMEM] + [VMEM] * 7,
        out_specs=[HBM] + [VMEM] * 6,
        scratch_shapes=[
            pltpu.VMEM((SLOT, width), BF),
            pltpu.VMEM((width, SLOT), BF),
            pltpu.VMEM((SLOT, 128), BF),
            pltpu.VMEM((SLOT, SLOT), F32),
            pltpu.VMEM((SLOT, SLOT), F32),
            pltpu.VMEM((HEADS * PREFIX, SLOT), F32),
            pltpu.VMEM((HEADS // GROUP, 8, SLOT), F32),
            pltpu.VMEM((8, SLOT), F32),
            pltpu.VMEM((width, SLOT), F32),
            pltpu.VMEM((HEADS, SLOT), F32),
            pltpu.VMEM((SLOT, SLOT), BF),
            pltpu.VMEM((SLOT, SLOT), BF),
            pltpu.SemaphoreType.DMA((2,)),
        ],
        compiler_params=params,
        name="attend_forward",
    )(lengths, key_mask.reshape(1, SLOT), tokens, w_query, w_key, w_value, prefix_key, prefix_value)

    vectors = jnp.stack([norm1_gain, norm1_shift, norm2_gain, norm2_shift] * 2).astype(F32)
    output, lower, grad_t, centre = pl.pallas_call(
        middle_kernel,
        out_shape=[square, shape((SLOT, width), F32), square, shape((HEADS * 16, SLOT), BF)],
        in_specs=[VMEM] * 9,
        out_specs=[VMEM] * 4,
        scratch_shapes=[
            pltpu.VMEM((SLOT, width), F32),
            pltpu.VMEM((SLOT, 1), F32),
            pltpu.VMEM((SLOT, width), BF),
            pltpu.VMEM((SLOT, width), F32),
            pltpu.VMEM((2, SLOT, hidden), BF),
            pltpu.VMEM((shards, SLOT, hidden), BF),
        ],
        compiler_params=params,
        name="feed_forward",
    )(tokens, context_t, inverse, w_output, vectors, w_in_all, b_all, w_out_all, out_grad)

    input_grad, prefix_grads = pl.pallas_call(
        backward_kernel,
        out_shape=[square, shape((2 * PREFIX, width), F32)],
        in_specs=[HBM] + [VMEM] * 12,
        out_specs=[VMEM] * 2,
        scratch_shapes=[
            pltpu.VMEM((width, SLOT), BF),
            pltpu.VMEM((width, SLOT), BF),
            pltpu.VMEM((width, SLOT), BF),
            pltpu.VMEM((width, SLOT), F32),
            pltpu.VMEM((2, SLOT, SLOT), BF),
            pltpu.SemaphoreType.DMA((2,)),
        ],
        compiler_params=params,
        name="attend_backward",
    )(weights, weights_prefix, query_t, key_t, value, grad_t, centre, prefix_key, prefix_value,
      lower, w_query, w_key, w_value)

    whole = lax.psum(prefix_grads, ("dp", "mp"))
    share = width // shards
    part = lax.dynamic_slice_in_dim(whole, lax.axis_index("mp") * share, share, 1)
    return output, input_grad, part[:PREFIX], part[PREFIX:]


def solution(mesh):
    in_specs = (
        P(("dp", "mp"), None), P(("dp", "mp")), P(("dp", "mp")), P(), P(), P(), P(), P(), P(),
        P(None, "mp"), P("mp"), P("mp", None), P(), P(), P(), P(), P(("dp", "mp"), None),
    )
    out_specs = (P(("dp", "mp"), None), P(("dp", "mp"), None), P(None, "mp"), P(None, "mp"))
    return jax.shard_map(local, mesh=mesh, in_specs=in_specs, out_specs=out_specs, check_vma=False)
```

time: 943 us -> 391 us (0.41)
  matrix products: 364 us -> 0 us
  waiting for transfers between devices: 367 us -> 205 us
  Pallas kernels: 0 us -> 161 us
  other arithmetic: 111 us -> 0.62 us
  local copies, waits for them, and re-layouts: 75.9 us -> 2.3 us
    dot_general x25 -> x0, matrix products: 364 us -> none  [the longest x4 89.8 us: block_scores(): jnp.einsum('qhd,khd->hqk', query_block, keys, preferred_element_type=jnp....]
    pallas_call x0 -> x3, Pallas kernels: none -> 161 us  [the longest x1 71.9 us: local(): pl.pallas_call(middle_kernel, out_shape=[square, shape((SLOT, width), F32...]
    reduce_scatter x2 -> x0, waiting for transfers between devices: 139 us -> none  [the longest x1 71.2 us: local(): lax.psum_scatter(product_back(pre_grad, w_in).astype(jnp.bfloat16), 'mp',...]
    convert_element_type x9 -> x2, other arithmetic: 63.3 us -> 0.62 us  [the longest x1 0.62 us: local(): jnp.stack([norm1_gain, norm1_shift, norm2_gain, norm2_shift] * 2)]
    all_gather x2, waiting for transfers between devices: 119 us -> 75.8 us  [the longest x1 59.9 us: local(): w_out_all = lax.all_gather(w_out, 'mp', axis=0)]
    reduce_sum x7 -> x0, other arithmetic: 42.4 us -> none  [the longest x2 30.1 us: one_block(): total = jnp.sum(weights, axis=-1, keepdims=True)]
    unnamed x89 -> x11, local copies, waits for them, and re-layouts: 35.4 us -> 0.68 us
    psum x1, waiting for transfers between devices: 109 us -> 128 us  [local(): whole = lax.psum(prefix_grads, ('dp', 'mp'))]
  transfers between devices with their start and end apart: 5 -> 3, of which waited for: 5 -> 3; matrix products, arithmetic and copies ran while one was open for 3% -> 0% of each run, Pallas kernels for 0% -> 10%
where the time goes in v1:
time: 391 us; the launch traced here: 390 us
  waiting for transfers between devices  205 us (52%)
  Pallas kernels  161 us (41%)
  between operations  14.5 us (4%)
  blocking collectives  6.22 us (2%)
    psum x1, waiting for transfers between devices, local(): whole = lax.psum(prefix_grads, ('dp', 'mp'))  128 us
    pallas_call x1, Pallas kernels, local(): pl.pallas_call(middle_kernel, out_shape=[square, shape((SLOT, width), F32...  71.9 us
    all_gather x1, waiting for transfers between devices, local(): w_out_all = lax.all_gather(w_out, 'mp', axis=0)  59.9 us
    pallas_call x1, Pallas kernels, local(): pl.pallas_call(backward_kernel, out_shape=[square, shape((2 * PREFIX, wid...  51.2 us
    pallas_call x1, Pallas kernels, local(): pl.pallas_call(forward_kernel, out_shape=[shape((HEADS, SLOT, SLOT), BF),...  38.3 us
    all_gather x1, waiting for transfers between devices, local(): w_in_all = lax.all_gather(w_in, 'mp', axis=0)  15.9 us
  transfers between devices with their start and end apart: 3, of which 3 were waited for; matrix products, arithmetic and copies ran while one was open for 0% of the time, Pallas kernels for 10%

profile of v1, /device:TPU:0, one launch (start us, length us, event | category | flops | bytes accessed | tf_op | source)
XLA Modules:
  0.0 390.3 jit_solution(17834723763816481549)
XLA Ops:
  7.2 0.0 copy-start
  7.2 0.0 copy-start.1
  7.2 0.0 copy-start.2
  7.2 0.0 copy-start.3
  7.2 0.0 copy-start.4
  7.2 0.0 all-gather.6.cloned.1.call-start
  7.3 0.7 all-gather.6.cloned.1.call-update
  8.0 0.0 all-gather.8.cloned.1.call-start
  8.0 0.7 all-gather.8.cloned.1.call-update
  8.7 0.0 all-reduce.2.cloned.1.call-start
  9.4 0.0 copy-done
  9.4 6.2 %all-gather.1 = f32[4096]{0:T(1024)S(1)} all-gather(f32[1024]{0:T(1024)S(1)} %convert_element_type.7), channel_id=4, replica_groups=mesh['dp'=8,'mp'=4] {'mp'}, dimensions={0}, use_global_device_ids=true | all-gather | bytes 20480 | tf_op jit(solution)/shard_map/all_gather | solution.py:416
  15.6 0.0 copy-done.1
  15.7 0.0 copy-done.2
  15.7 0.0 copy-done.3
  15.7 0.0 copy-done.4
  15.7 0.1 stack.23
  15.8 0.6 convert_element_type.6.vectors
  16.4 38.3 %attend_forward.1 = (bf16[16,1024,1024]{2,1,0:T(8,128)(2,1)}, bf16[1024,1024]{1,0:T(8,128)(2,1)}, bf16[1024,1024]{1,0:T(8,128)(2,1)}, bf16[1024,1024]{1,0:T(8,12...) custom-call(s32[1]{0:T(128)S(6)} %copy.22.length, s32[1,1024]{1,0:T(1,128)} %bitcast.5, ...), custom_call_target="tpu_custom_call" | custom-call | tf_op jit(solution)/shard_map/attend_forward/pallas_call | solution.py:419
  54.7 15.9 %all-gather.6.cloned.1.call-done = bf16[4096,1024]{1,0:T(8,128)(2,1)} async-done(((bf16[1024,1024]{1,0:T(8,128)(2,1)}), bf16[4096,1024]{1,0:T(8,128)(2,1)}) %all-gather.6.cloned.1.call-update) | async-done | bytes 8388624 | tf_op jit(solution)/shard_map/all_gather | solution.py:414
  70.6 59.9 %all-gather.8.cloned.1.call-done = bf16[4096,1024]{1,0:T(8,128)(2,1)} async-done(((bf16[1024,1024]{1,0:T(8,128)(2,1)}), bf16[4096,1024]{1,0:T(8,128)(2,1)}) %all-gather.8.cloned.1.call-update) | async-done | bytes 8388624 | tf_op jit(solution)/shard_map/all_gather | solution.py:415
  130.5 0.7 broadcast.4.b_in
  131.2 71.9 %feed_forward.1 = (bf16[1024,1024]{1,0:T(8,128)(2,1)}, f32[1024,1024]{1,0:T(8,128)}, bf16[1024,1024]{1,0:T(8,128)(2,1)}, bf16[256,1024]{1,0:T(8,128)(2,1)}) custom-call(bf16[1024,1024]{1,0:T(8,128)(2,1)} %tokens.3, bf16[1024,1024]{1,0:T(8,128)(2,1)} %get-tuple-element.17.context_t, f32[16,1024]{1,0:T(8,128)} %get-tuple-element.18.inverse, ...), custom_call_target="tpu_custom_call" | custom-call | tf_op jit(solution)/shard_map/feed_forward/pallas_call | solution.py:445
  203.1 51.2 %attend_backward.1 = (bf16[1024,1024]{1,0:T(8,128)(2,1)}, f32[128,1024]{1,0:T(8,128)}) custom-call(bf16[16,1024,1024]{2,1,0:T(8,128)(2,1)} %get-tuple-element.20.weights_hbm, bf16[1024,1024]{1,0:T(8,128)(2,1)} %get-tuple-element.21.weights_prefix, bf16[1024,1024]{1,0:T(8,128)(2,1)} %get-tuple-element.22.query_t, bf16[1024,1024]{1,0:T(8,128)(2,1)} %get-tuple-element.23.key_t, ...), custom_call_target="tpu_custom_call" | custom-call | tf_op jit(solution)/shard_map/attend_backward/pallas_call | solution.py:462
  254.2 0.0 all-reduce.2.cloned.1.call-update
  254.3 128.0 %all-reduce.2.cloned.1.call-done = f32[128,1024]{1,0:T(8,128)} async-done(((f32[128,1024]{1,0:T(8,128)}), f32[128,1024]{1,0:T(8,128)}) %all-reduce.2.cloned.1.call-update) | async-done | bytes 524304 | tf_op jit(solution)/shard_map/psum | solution.py:480
  382.3 1.5 fusion
  (6 shorter events, 0.0 us)
Async XLA Ops:
  7.2 2.2 copy-start
  7.2 8.5 %copy-start.1 = (bf16[1024]{0:T(1024)(128)(2,1)S(1)}, bf16[1024]{0:T(1024)(128)(2,1)}, u32[]{:S(2)}) copy-start(bf16[1024]{0:T(1024)(128)(2,1)} %param.24) | copy-start | bytes 6148
  7.2 8.5 %copy-start.2 = (bf16[1024]{0:T(1024)(128)(2,1)S(1)}, bf16[1024]{0:T(1024)(128)(2,1)}, u32[]{:S(2)}) copy-start(bf16[1024]{0:T(1024)(128)(2,1)} %param.25) | copy-start | bytes 6148
  7.2 8.5 %copy-start.3 = (bf16[1024]{0:T(1024)(128)(2,1)S(1)}, bf16[1024]{0:T(1024)(128)(2,1)}, u32[]{:S(2)}) copy-start(bf16[1024]{0:T(1024)(128)(2,1)} %param.29) | copy-start | bytes 6148
  7.2 8.5 %copy-start.4 = (bf16[1024]{0:T(1024)(128)(2,1)S(1)}, bf16[1024]{0:T(1024)(128)(2,1)}, u32[]{:S(2)}) copy-start(bf16[1024]{0:T(1024)(128)(2,1)} %param.30) | copy-start | bytes 6148
  7.2 63.4 %all-gather.6.cloned.1.call-start = ((), (), s32[]{:S(2)}) async-start(), calls=%async_computation.1 | async-start | bytes 10485760 | tf_op jit(solution)/shard_map/all_gather | solution.py:414
  8.0 122.6 %all-gather.8.cloned.1.call-start = ((), (), s32[]{:S(2)}) async-start(), calls=%async_computation.2 | async-start | bytes 10485760 | tf_op jit(solution)/shard_map/all_gather | solution.py:415
  8.7 373.6 %all-reduce.2.cloned.1.call-start = ((), (), s32[]{:S(2)}) async-start(), calls=%async_computation | async-start | bytes 1048576 | tf_op jit(solution)/shard_map/psum | solution.py:480
Sparse Core Ops, SparseCore 0:
  9.6 60.9 all-gather.5
  72.2 58.2 all-gather.7
  254.4 127.8 all-reduce.1
